TPU v7x, 256 devices: a whole 4x4x8 slice. The times are simulated.
256 devices in a mesh: ctx: 32 (over z, x), head: 8 (over y, core).
Axes of the slice: x: 4, y: 4, z: 8, core: 2. Of those that a mesh axis runs over, the one named last changes fastest.
Arguments:
- queries: bfloat16 [4096, 4096], P('ctx', 'head'), may hold values from -0.625 to 0.625
- key_vectors: bfloat16 [4096, 4096], P('ctx', 'head'), may hold values from -1.75 to 1.75
- value_vectors: bfloat16 [4096, 4096], P('ctx', 'head'), may hold values from -6 to 6
- out_grad: bfloat16 [4096, 6144], P('ctx', 'head'), may hold values from -1.25 to 1.25
- out_weight: bfloat16 [6144, 4096], P(None, 'head'), may hold values from -0.09375 to 0.09375
- decay_rate: float32 [32], P('head'), may hold values from 2.4414063e-05 to 0.08, as said below
Outputs:
- query_grad: bfloat16 [4096, 4096], P('ctx', 'head')
- key_grad: bfloat16 [4096, 4096], P('ctx', 'head')
- value_grad: bfloat16 [4096, 4096], P('ctx', 'head')
- weight_grad: float32 [6144, 4096], P('ctx', 'head')
Inputs may be any that keep to these rules, and one draw needn't show every extreme that they name: decay_rate[h] is the rate r of head h: its state is multiplied by exp(-r) at each position.
All inputs are finite; a program needn't handle non-finite values.
Results may differ from a plain program's by a relative error of at most 0.0064.
Values may be sent and summed in bfloat16 or wider, within the bound.
A program may use at most 128 MiB of HBM per device.

v0:
```python
import jax
import jax.numpy as jnp
from jax import lax
from jax.sharding import PartitionSpec as P

E = 128


def entering(part, axis, combine, identity, reverse):
    count = lax.axis_size(axis)
    place = lax.axis_index(axis)
    ahead = count - 1 - place if reverse else place
    gathered = jax.tree.map(lambda a: lax.all_gather(a, axis), part)
    state = jax.tree.map(lambda a, e: jnp.zeros_like(a) + jnp.asarray(e, a.dtype), part, identity)

    def one(lap, state):
        source = count - 1 - lap if reverse else lap
        return combine(
            state, jax.tree.map(lambda a: lax.dynamic_index_in_dim(a, source, 0, False), gathered)
        )

    return lax.fori_loop(0, ahead, one, state)


def chain_link(earlier, later):
    return (earlier[0] * later[0], later[0][:, None, None] * earlier[1] + later[1])


def multiply(form, left, right):
    return jnp.einsum(form, left, right, preferred_element_type=jnp.float32)


def local(queries, key_vectors, value_vectors, out_grad, out_weight, decay_rate):
    length = queries.shape[0]
    columns_here = queries.shape[1]
    heads_here = columns_here // E
    block_rows = min(length, 512)
    blocks = length // block_rows
    full_grad = lax.all_gather(out_grad, "head", axis=1, tiled=True)
    head_grad = jnp.dot(full_grad, out_weight, preferred_element_type=jnp.float32).astype(
        jnp.bfloat16
    )

    def split_heads(tensor):
        return (
            tensor.reshape(length, heads_here, E)
            .transpose(1, 0, 2)
            .reshape(heads_here, blocks, block_rows, E)
        )

    def join_heads(tensor):
        return (
            tensor.reshape(heads_here, length, E)
            .transpose(1, 0, 2)
            .reshape(length, columns_here)
            .astype(jnp.bfloat16)
        )

    q_blocks = split_heads(queries)
    k_blocks = split_heads(key_vectors)
    v_blocks = split_heads(value_vectors)
    g_blocks = split_heads(head_grad)
    offsets = jnp.arange(block_rows, dtype=jnp.float32)
    distance = offsets[:, None] - offsets[None, :]
    weights = jnp.where(
        distance[None] >= 0,
        jnp.exp(-decay_rate[:, None, None] * jnp.maximum(distance, 0.0)[None]),
        0.0,
    )
    in_decay = jnp.exp(-decay_rate[:, None] * (offsets + 1.0)[None])[:, None, :, None]
    out_decay = jnp.exp(-decay_rate[:, None] * (block_rows - 1.0 - offsets)[None])[:, None, :, None]
    back_decay = jnp.exp(-decay_rate[:, None] * (block_rows - offsets)[None])[:, None, :, None]
    tok_decay = jnp.exp(-decay_rate[:, None] * offsets[None])[:, None, :, None]
    step_decay = jnp.exp(-decay_rate * block_rows)[:, None, None]
    scores = (multiply("hnte,hnse->hnts", q_blocks, k_blocks) * weights[:, None]).astype(
        jnp.bfloat16
    )
    grad_scores = (multiply("hntf,hnsf->hnts", g_blocks, v_blocks) * weights[:, None]).astype(
        jnp.bfloat16
    )
    keys_decayed = (k_blocks.astype(jnp.float32) * out_decay).astype(jnp.bfloat16)
    queries_decayed = (q_blocks.astype(jnp.float32) * tok_decay).astype(jnp.bfloat16)
    kv_terms = multiply("hnse,hnsf->nhef", keys_decayed, v_blocks)
    qg_terms = multiply("hnte,hntf->nhef", queries_decayed, g_blocks)

    def advance(running, term_rows):
        return (step_decay * running + term_rows, running)

    zero_state = jnp.zeros((heads_here, E, E), jnp.float32)
    local_end, starts = lax.scan(advance, zero_state, kv_terms)
    local_begin, ends = lax.scan(advance, zero_state, qg_terms, reverse=True)
    device_decay = jnp.exp(-decay_rate * length)
    identity = (jnp.ones((heads_here,), jnp.float32), zero_state)
    _, state_in = entering((device_decay, local_end), "ctx", chain_link, identity, False)
    _, grad_in = entering((device_decay, local_begin), "ctx", chain_link, identity, True)
    block_index = jnp.arange(blocks, dtype=jnp.float32)
    start_decay = jnp.exp(-decay_rate[None, :] * (block_index * block_rows)[:, None])
    end_decay = jnp.exp(-decay_rate[None, :] * ((blocks - 1.0 - block_index) * block_rows)[:, None])
    starts = (starts + start_decay[:, :, None, None] * state_in[None]).astype(jnp.bfloat16)
    ends = (ends + end_decay[:, :, None, None] * grad_in[None]).astype(jnp.bfloat16)
    attention_out = in_decay * multiply("hnte,nhef->hntf", q_blocks, starts)
    attention_out = attention_out + multiply("hnts,hnsf->hntf", scores, v_blocks)
    query_grad = in_decay * multiply("hntf,nhef->hnte", g_blocks, starts)
    query_grad = query_grad + multiply("hnts,hnse->hnte", grad_scores, k_blocks)
    key_grad = back_decay * multiply("hnsf,nhef->hnse", v_blocks, ends)
    key_grad = key_grad + multiply("hnts,hnte->hnse", grad_scores, q_blocks)
    value_grad = back_decay * multiply("hnse,nhef->hnsf", k_blocks, ends)
    value_grad = value_grad + multiply("hnts,hntf->hnsf", scores, g_blocks)
    attention_bf = join_heads(attention_out)
    weight_grad = lax.psum_scatter(
        lax.dot_general(
            full_grad, attention_bf, (((0,), (0,)), ((), ())), preferred_element_type=jnp.float32
        ),
        "ctx",
        scatter_dimension=0,
        tiled=True,
    )
    return (join_heads(query_grad), join_heads(key_grad), join_heads(value_grad), weight_grad)


def solution(mesh):
    in_specs = (
        P("ctx", "head"),
        P("ctx", "head"),
        P("ctx", "head"),
        P("ctx", "head"),
        P(None, "head"),
        P("head"),
    )
    out_specs = (P("ctx", "head"), P("ctx", "head"), P("ctx", "head"), P("ctx", "head"))
    return jax.shard_map(local, mesh=mesh, in_specs=in_specs, out_specs=out_specs, check_vma=False)
```

profile of v0, /device:TPU:16, one launch (start us, length us, event | category | flops | bytes accessed | tf_op | source)
XLA Modules:
  0.0 485.4 jit_solution(14921316918511483909)
XLA Ops:
  9.0 1.3 dynamic-slice.2
  12.9 25.6 %all-gather.7.cloned.1.call-done = bf16[128,6144]{1,0:T(8,128)(2,1)} async-done(((bf16[128,768]{1,0:T(8,128)(2,1)}), bf16[128,6144]{1,0:T(8,128)(2,1)}) %all-gather.7.cloned.1.call-update) | async-done | bytes 1572880 | tf_op jit(solution)/shard_map/all_gather | solution.py:39
  38.5 4.4 convolution_convert_fusion
  44.1 75.7 %all-reduce = f32[128]{0:T(128)S(1)} all-reduce(f32[128]{0:T(128)S(1)} %get-tuple-element.201), channel_id=2, replica_groups=mesh['ctx'=32,'head'=8] {'ctx'}, use_global_device_ids=true, to_apply=%add | all-reduce | flops 128 | bytes 1024
  120.3 21.2 %all-gather.9.cloned.1.call-done = f32[128,128,128]{2,1,0:T(8,128)} async-done(((f32[4,128,128]{2,1,0:T(8,128)}), f32[128,128,128]{2,1,0:T(8,128)}) %all-gather.9.cloned.1.call-update) | async-done | bytes 8388624 | tf_op jit(solution)/shard_map/all_gather | solution.py:13
  142.1 6.3 %convolution_bitcast_fusion = f32[6144,512]{0,1:T(8,128)} fusion(bf16[128,512]{0,1:T(8,128)(2,1)S(1)} %bitcast.158, bf16[128,6144]{1,0:T(8,128)(2,1)S(1)} %copy-done.1), kind=kOutput, calls=%fused_computation.4 | convolution fusion | flops 805306368 | bytes 14286848 | tf_op jit(solution)/shard_map/dot_general | solution.py:111
  148.4 12.6 %copy.88 = f32[6144,512]{1,0:T(8,128)} copy(f32[6144,512]{0,1:T(8,128)} %convolution_bitcast_fusion) | data formatting | bytes 25165824
  162.5 76.9 %all-gather.11.cloned.1.call-done = f32[128,128,128]{2,1,0:T(8,128)} async-done(((f32[4,128,128]{2,1,0:T(8,128)}), f32[128,128,128]{2,1,0:T(8,128)}) %all-gather.11.cloned.1.call-update) | async-done | bytes 8388624 | tf_op jit(solution)/shard_map/all_gather | solution.py:13
  239.5 34.3 %while.17 = (s32[]{:T(128)}, f32[4,128,128]{2,1,0:T(8,128)S(1)}, s32[]{:T(128)}, f32[32,4]{1,0:T(8,128)S(1)}, f32[32,4,128,128]{3,2,1,0:T(8,128)}, /*index=5*/s32[]{:T(128)}, s32[]{:T(128)}, s32[]{:T(128)}, s32[]{:T(128)}) while((s32[]{:T(128)}, f32[4,128,128]{2,1,0:T(8,128)S(1)}, s32[]{:T(128)}, f32[32,4]{1,0:T(8,128)S(1)}, ...), condition=%wide.region_3.4_spmd, body=%wide.region_2.3_spmd.sunk | while | flops 131078 | bytes 786635 | solution.py:22
  239.5 1.1 bitcast_add_fusion.5
  240.6 1.1 bitcast_add_fusion.5
  241.8 1.1 bitcast_add_fusion.5
  252.8 1.1 bitcast_add_fusion.5
  258.3 1.1 bitcast_add_fusion.5
  259.4 1.1 bitcast_add_fusion.5
  260.6 1.1 bitcast_add_fusion.5
  263.9 1.1 bitcast_add_fusion.5
  265.0 1.1 bitcast_add_fusion.5
  267.2 1.1 bitcast_add_fusion.5
  268.3 1.1 bitcast_add_fusion.5
  269.4 1.1 bitcast_add_fusion.5
  271.6 1.1 bitcast_add_fusion.5
  272.7 1.1 bitcast_add_fusion.5
  276.3 202.5 %reduce-scatter.4.cloned.1.call-done = f32[192,512]{1,0:T(8,128)} async-done(((f32[6144,512]{1,0:T(8,128)}), f32[192,512]{1,0:T(8,128)}) %reduce-scatter.4.cloned.1.call-update) | async-done | bytes 393232
  (91 shorter events, 28.3 us)
Async XLA Ops:
  7.2 4.6 copy-start
  7.2 35.8 %copy-start.2 = (bf16[128,512]{1,0:T(8,128)(2,1)S(1)}, bf16[128,512]{1,0:T(8,128)(2,1)}, u32[]{:S(2)}) copy-start(bf16[128,512]{1,0:T(8,128)(2,1)} %param.10) | copy-start | bytes 393220
  7.2 31.3 %all-gather.7.cloned.1.call-start = ((), (), s32[]{:S(2)}) async-start(), calls=%async_computation.1 | async-start | bytes 1769472 | tf_op jit(solution)/shard_map/all_gather | solution.py:39
  7.9 133.6 %all-gather.9.cloned.1.call-start = ((), (), s32[]{:S(2)}) async-start(), calls=%async_computation.2 | async-start | bytes 8650752 | tf_op jit(solution)/shard_map/all_gather | solution.py:13
  12.8 226.6 %all-gather.11.cloned.1.call-start = ((), (), s32[]{:S(2)}) async-start(), calls=%async_computation.3 | async-start | bytes 8650752 | tf_op jit(solution)/shard_map/all_gather | solution.py:13
  38.5 103.6 %copy-start.1 = (bf16[128,6144]{1,0:T(8,128)(2,1)S(1)}, bf16[128,6144]{1,0:T(8,128)(2,1)}, u32[]{:S(2)}) copy-start(bf16[128,6144]{1,0:T(8,128)(2,1)} %all-gather.7.cloned.1.call-done) | copy-start | bytes 4718596
  44.1 434.8 %reduce-scatter.4.cloned.1.call-start = ((), (), s32[]{:S(2)}) async-start(), calls=%async_computation.4 | async-start | bytes 12976128
Sparse Core Ops, SparseCore 0:
  9.9 28.5 all-gather.6
  41.7 99.8 all-gather.8
  144.1 95.3 all-gather.10
  244.0 234.7 reduce-scatter.3
where the time goes:
time: 487 us; the launch traced here: 485 us
  waiting for transfers between devices  327 us (67%)
  blocking collectives  75.7 us (16%)
  other arithmetic  33.9 us (7%)
  local copies, waits for them, and re-layouts  17.9 us (4%)
  matrix products  15.1 us (3%)
  between operations  14.6 us (3%)
    unnamed x5, waiting for transfers between devices  203 us
    all_gather x2, waiting for transfers between devices, entering(): gathered = jax.tree.map(lambda a: lax.all_gather(a, axis), part)  98.2 us
    unnamed x1, blocking collectives  75.7 us
    add x31, other arithmetic, chain_link(): later[0][:, None, None] * earlier[1] + later[1]  33 us
    all_gather x1, waiting for transfers between devices, local(): full_grad = lax.all_gather(out_grad, 'head', axis=1, tiled=True)  25.6 us
    unnamed x12, local copies, waits for them, and re-layouts  16.2 us
  transfers between devices with their start and end apart: 4, of which 4 were waited for; matrix products, arithmetic and copies ran while one was open for 14% of the time, Pallas kernels for 0%

commit v1 on v0

v1 whole, which is shorter than its diff:
```python
import functools

import jax
import jax.numpy as jnp
from jax import lax
from jax.experimental import pallas as pl
from jax.experimental.pallas import tpu as pltpu
from jax.sharding import PartitionSpec as P

E = 128
X = 4
MESH = pl.DeviceIdType.MESH
F32 = jnp.float32
BF16 = jnp.bfloat16


def dot(a, b, ca=1, cb=0):
    return lax.dot_general(a, b, (((ca,), (cb,)), ((), ())), preferred_element_type=F32)


def kernel(Z, Y, r_ref, q_hbm, k_hbm, v_hbm, og_hbm, w_hbm, qg_ref, kg_ref, vg_ref, wg_ref,
           q, k, v, w, fg, gz, gzt, hg, hacc, sc, gs, ts, tx, rs, rz, ss, st, acc, ab, dws, dwr,
           local_sem, g_send, g_recv, p_send, p_recv, t_send, t_recv, r_send, r_recv,
           s_send, s_recv, a_send, a_recv, d_send, d_recv):
    B = q.shape[0]
    D8 = fg.shape[2]
    CH = D8 // X
    H = 2 * Y
    PIECE = B // H
    ctx = lax.axis_index("ctx")
    h = lax.axis_index("head")
    z, x = ctx // X, lax.rem(ctx, X)
    y, c = h // 2, lax.rem(h, 2)

    def at_z(zz):
        return (lax.rem(zz + Z, Z) * X + x, h)

    def at_x(xx):
        return (z * X + xx, h)

    def yhead(dy, cc):
        return lax.rem(y + dy + Y, Y) * 2 + cc

    def at_h(hh):
        return (ctx, hh)

    sib = 1 - c

    def remote(src, dst, send, recv, to):
        return pltpu.make_async_remote_copy(
            src_ref=src, dst_ref=dst, send_sem=send, recv_sem=recv, device_id=to, device_id_type=MESH)

    loads = [pltpu.make_async_copy(a, b, local_sem.at[i]) for i, (a, b) in enumerate(
        ((k_hbm, k), (v_hbm, v), (q_hbm, q), (og_hbm, fg.at[h]), (w_hbm, w)))]
    for load in loads:
        load.start()
    barrier = pltpu.get_barrier_semaphore()
    peers = ([at_z(z + d) for d in range(1, Z)] + [at_x(lax.rem(x + o, X)) for o in range(1, X)]
             + [at_h(yhead(1, c)), at_h(yhead(-1, c)), at_h(yhead(0, sib))])
    for peer in peers:
        pl.semaphore_signal(barrier, inc=1, device_id=peer, device_id_type=MESH)

    rows = lax.broadcasted_iota(jnp.int32, (B, E), 0).astype(F32)
    dist = (lax.broadcasted_iota(jnp.int32, (B, B), 0)
            - lax.broadcasted_iota(jnp.int32, (B, B), 1)).astype(F32)

    def head(ref, j):
        return ref[:, j * E:(j + 1) * E]

    def weights(j):
        return jnp.where(dist >= 0, jnp.exp(-r_ref[j] * jnp.maximum(dist, 0.0)), 0.0)

    def power(rate, count):
        return jnp.exp(jnp.full((1, E), -rate * count, F32))

    def scan_send(g):
        for o in range(1, X):
            peer = lax.rem(x + o, X)
            remote(ts.at[g, peer], tx.at[g, x], t_send.at[g, o - 1], t_recv.at[g, o - 1], at_x(peer)).start()
        tx[g, x] = ts[g, x]

    r_own = r_ref[x]

    def scan_rows(g):
        for o in range(1, X):
            src = lax.rem(x - o + X, X)
            remote(ts.at[g, src], tx.at[g, src], t_send.at[g, o - 1], t_recv.at[g, o - 1], at_x(src)).wait_recv()
        total = jnp.zeros((E, E), F32)
        for xx in range(X):
            away = xx if g else X - 1 - xx
            total = total + power(r_own, float(B * away)) * tx[g, xx].astype(F32)
        rs[g] = total.astype(BF16)
        for d in range(1, Z):
            there = z - d if g else z + d

            @pl.when((there >= 0) & (there < Z))
            def _():
                remote(rs.at[g], rz.at[g, z], r_send.at[g, d - 1], r_recv.at[g, d - 1], at_z(there)).start()

    def scan_finish(g):
        acc[...] = jnp.zeros((E, E), F32)
        for d in range(1, Z):
            src = z + d if g else z - d

            @pl.when((src >= 0) & (src < Z))
            def _():
                remote(rs.at[g], rz.at[g, src], r_send.at[g, d - 1], r_recv.at[g, d - 1], at_z(src)).wait_recv()
                acc[...] += power(r_own, float(X * B * (d - 1))) * rz[g, src].astype(F32)

        state = acc[...]
        step = power(r_own, float(B))
        for xx in (reversed(range(X)) if g else range(X)):
            ss[g, xx] = state.astype(BF16)
            state = step * state + tx[g, xx].astype(F32)
        for o in range(1, X):
            peer = lax.rem(x + o, X)
            remote(ss.at[g, peer], st.at[g, x], s_send.at[g, o - 1], s_recv.at[g, o - 1], at_x(peer)).start()
        st[g, x] = ss[g, x]

    def scan_wait(g):
        for o in range(1, X):
            src = lax.rem(x - o + X, X)
            remote(ss.at[g, src], st.at[g, src], s_send.at[g, o - 1], s_recv.at[g, o - 1], at_x(src)).wait_recv()

    def piece(n, hh, half=None):
        if n == 0:
            if half is None:
                return fg.at[hh]
            return fg.at[hh, half * (B // 2):(half + 1) * (B // 2), :]
        mine = pl.ds(pl.multiple_of(hh * PIECE, PIECE), PIECE)
        if half is None:
            return gz.at[:, mine, :]
        return gz.at[half * (Z // 2):(half + 1) * (Z // 2), mine, :]

    def hop(n, hh, half, i, to):
        ref = piece(n, hh, half)
        return remote(ref, ref, g_send.at[n, i], g_recv.at[n, i], at_h(to))

    up, down = yhead(1, c), yhead(-1, c)
    far = yhead(2, c)
    across = yhead(0, sib)

    def gather_start(n):
        hop(n, h, 0, 0, up).start()
        hop(n, h, 1, 1, down).start()
        hop(n, h, None, 6, across).start()
        hop(n, h, 1, 2, up).start()
        hop(n, h, 0, 3, down).start()

    def gather_forward(n):
        hop(n, down, 0, 0, up).wait_recv()
        hop(n, down, 0, 4, up).start()
        hop(n, up, 1, 1, down).wait_recv()
        hop(n, up, 1, 5, down).start()

    def gather_near(n):
        hop(n, down, 1, 2, up).wait_recv()
        hop(n, down, None, 7, across).start()
        hop(n, up, 0, 3, down).wait_recv()
        hop(n, up, None, 8, across).start()

    def gather_far(n):
        hop(n, far, 0, 4, up).wait_recv()
        hop(n, far, 1, 5, down).wait_recv()
        hop(n, far, None, 9, across).start()

    def gather_across(n, i):
        hh = yhead((0, -1, 1, 2)[i], sib)
        hop(n, hh, None, 6 + i, across).wait_recv()
        return hh

    my_piece = pl.ds(pl.multiple_of(h * PIECE, PIECE), PIECE)

    def pass_piece(zz):
        @pl.when(zz != z)
        def _():
            remote(fg.at[zz, my_piece, :], gz.at[z, my_piece, :], p_send.at[zz], p_recv.at[z], at_z(zz)).start()

        @pl.when(zz == z)
        def _():
            gz[z, my_piece, :] = fg[zz, my_piece, :]

    hops = ((Z // 2, Z - 1 - Z // 2), (Z - 1 - Z // 2, Z // 2))

    def ring(s):
        for p in range(2):
            for way in range(2):
                sign = -1 if way else 1
                if 0 < s <= hops[p][way]:
                    came = lax.rem(z - sign * s + Z, Z)
                    remote(ab.at[p, came], ab.at[p, came], a_send.at[p, way, s - 1],
                           a_recv.at[p, way, s - 1], at_z(z + sign)).wait_recv()
                if s < hops[p][way]:
                    block = lax.rem(z - sign * s + Z, Z)
                    remote(ab.at[p, block], ab.at[p, block], a_send.at[p, way, s],
                           a_recv.at[p, way, s], at_z(z + sign)).start()

    for load in loads[:3]:
        load.wait()
    for j in range(X):
        decayed = (head(k, j).astype(F32) * jnp.exp(-r_ref[j] * (B - 1.0 - rows))).astype(BF16)
        ts[0, j] = dot(decayed, head(v, j), 0, 0).astype(BF16)
    loads[3].wait()
    pl.semaphore_wait(barrier, len(peers))

    scan_send(0)
    gather_start(0)
    pass_piece(h)
    for j in range(X):
        sc[j] = (dot(head(q, j), head(k, j), 1, 1) * weights(j)).astype(BF16)
    scan_rows(0)
    pass_piece(gather_across(0, 0))
    gather_forward(0)
    gather_near(0)
    pass_piece(down)
    pass_piece(up)
    pass_piece(gather_across(0, 1))
    pass_piece(gather_across(0, 2))
    scan_finish(0)
    gather_far(0)
    pass_piece(far)
    pass_piece(gather_across(0, 3))

    loads[4].wait()
    hacc[...] = jnp.zeros_like(hacc)

    def part(i, carry):
        hacc[...] += dot(fg[i], w[pl.ds(pl.multiple_of(i * D8, D8), D8), :])
        return carry

    lax.fori_loop(0, H, part, 0)
    hg[...] = hacc[...].astype(BF16)

    scan_wait(0)
    for j in range(X):
        inter = jnp.exp(-r_ref[j] * (rows + 1.0)) * dot(head(q, j), st[0, j])
        ab[j // 2, z, :, (j % 2) * E:(j % 2 + 1) * E] = (inter + dot(sc[j], head(v, j))).astype(BF16)
    ring(0)
    for j in range(X):
        decayed = (head(q, j).astype(F32) * jnp.exp(-r_ref[j] * rows)).astype(BF16)
        ts[1, j] = dot(decayed, head(hg, j), 0, 0).astype(BF16)
    scan_send(1)
    for zz in range(Z):
        @pl.when(zz != z)
        def _():
            remote(gz.at[zz, my_piece, :], gz.at[zz, my_piece, :], p_send.at[zz], p_recv.at[zz], at_z(zz)).wait_recv()
    gather_start(1)
    ring(1)
    scan_rows(1)
    gather_forward(1)
    ring(2)
    for j in range(X):
        gs[j] = (dot(head(hg, j), head(v, j), 1, 1) * weights(j)).astype(BF16)
        inter = jnp.exp(-r_ref[j] * (rows + 1.0)) * dot(head(hg, j), st[0, j], 1, 1)
        qg_ref[:, j * E:(j + 1) * E] = (inter + dot(gs[j], head(k, j))).astype(BF16)
    gather_near(1)
    ring(3)
    gather_far(1)
    for i in range(4):
        gather_across(1, i)
    for zz in range(Z):
        gzt[:, zz * B:(zz + 1) * B] = gz[zz].T
    scan_finish(1)
    for s in range(4, max(max(n) for n in hops) + 1):
        ring(s)

    def rows_of(xx):
        return gzt[pl.ds(pl.multiple_of(xx * CH, CH), CH), :]

    for p in range(2):
        right = ab[p].reshape(Z * B, 2 * E)
        for o in (2, 1, 3):
            peer = lax.rem(x + o, X)
            dws[p, o - 1] = dot(rows_of(peer), right).astype(BF16)
            remote(dws.at[p, o - 1], dwr.at[p, o - 1], d_send.at[p, o - 1], d_recv.at[p, o - 1], at_x(peer)).start()
    for p in range(2):
        wg_ref[:, p * 2 * E:(p + 1) * 2 * E] = dot(rows_of(x), ab[p].reshape(Z * B, 2 * E))
    scan_wait(1)
    for j in range(X):
        back = jnp.exp(-r_ref[j] * (B - rows))
        kg_ref[:, j * E:(j + 1) * E] = (
            back * dot(head(v, j), st[1, j], 1, 1) + dot(gs[j], head(q, j), 0, 0)).astype(BF16)
        vg_ref[:, j * E:(j + 1) * E] = (
            back * dot(head(k, j), st[1, j]) + dot(sc[j], head(hg, j), 0, 0)).astype(BF16)
    for p in range(2):
        for o in (1, 3, 2):
            src = lax.rem(x - o + X, X)
            remote(dws.at[p, o - 1], dwr.at[p, o - 1], d_send.at[p, o - 1], d_recv.at[p, o - 1], at_x(src)).wait_recv()
            wg_ref[:, p * 2 * E:(p + 1) * 2 * E] += dwr[p, o - 1].astype(F32)

    for g in range(2):
        for o in range(1, X):
            remote(ts.at[g, 0], tx.at[g, 0], t_send.at[g, o - 1], t_recv.at[g, o - 1], at_x(x)).wait_send()
            remote(ss.at[g, 0], st.at[g, 0], s_send.at[g, o - 1], s_recv.at[g, o - 1], at_x(x)).wait_send()
        for d in range(1, Z):
            there = z - d if g else z + d

            @pl.when((there >= 0) & (there < Z))
            def _():
                remote(rs.at[g], rz.at[g, z], r_send.at[g, d - 1], r_recv.at[g, d - 1], at_z(there)).wait_send()
    for n in range(2):
        for i, half in enumerate((0, 1, 1, 0, 0, 1, None, None, None, None)):
            hop(n, h, half, i, up).wait_send()
    for zz in range(Z):
        @pl.when(zz != z)
        def _():
            remote(fg.at[zz, my_piece, :], gz.at[z, my_piece, :], p_send.at[zz], p_recv.at[z], at_z(zz)).wait_send()
    for p in range(2):
        for way in range(2):
            for s in range(hops[p][way]):
                remote(ab.at[p, z], ab.at[p, z], a_send.at[p, way, s], a_recv.at[p, way, s], at_z(z + 1)).wait_send()
        for o in range(1, X):
            remote(dws.at[p, o - 1], dwr.at[p, o - 1], d_send.at[p, o - 1], d_recv.at[p, o - 1], at_x(x)).wait_send()


def solution(mesh):
    Z, Y = mesh.shape["ctx"] // X, mesh.shape["head"] // 2
    H = 2 * Y

    def local(queries, key_vectors, value_vectors, out_grad, out_weight, decay_rate):
        B, C = queries.shape
        D8 = out_grad.shape[1]
        D = out_weight.shape[0]
        CH = D8 // X
        dma = pltpu.SemaphoreType.DMA
        vmem = pltpu.VMEM
        any_spec = pl.BlockSpec(memory_space=pl.ANY)
        return pl.pallas_call(
            functools.partial(kernel, Z, Y),
            out_shape=[jax.ShapeDtypeStruct((B, C), BF16)] * 3 + [jax.ShapeDtypeStruct((CH, C), F32)],
            in_specs=[pl.BlockSpec(memory_space=pltpu.SMEM)] + [any_spec] * 5,
            out_specs=[pl.BlockSpec(memory_space=pltpu.VMEM)] * 4,
            scratch_shapes=[
                vmem((B, C), BF16), vmem((B, C), BF16), vmem((B, C), BF16), vmem((D, C), BF16),
                vmem((H, B, D8), BF16), vmem((Z, B, D8), BF16), vmem((D8, Z * B), BF16),
                vmem((B, C), BF16), vmem((B, C), F32),
                vmem((X, B, B), BF16), vmem((X, B, B), BF16),
                vmem((2, X, E, E), BF16), vmem((2, X, E, E), BF16),
                vmem((2, E, E), BF16), vmem((2, Z, E, E), BF16),
                vmem((2, X, E, E), BF16), vmem((2, X, E, E), BF16), vmem((E, E), F32),
                vmem((2, Z, B, 2 * E), BF16),
                vmem((2, X - 1, CH, 2 * E), BF16), vmem((2, X - 1, CH, 2 * E), BF16),
                dma((5,)), dma((2, 10)), dma((2, 10)), dma((Z,)), dma((Z,)),
                dma((2, X - 1)), dma((2, X - 1)), dma((2, Z - 1)), dma((2, Z - 1)),
                dma((2, X - 1)), dma((2, X - 1)), dma((2, 2, Z // 2)), dma((2, 2, Z // 2)),
                dma((2, X - 1)), dma((2, X - 1)),
            ],
            compiler_params=pltpu.CompilerParams(
                collective_id=0, has_side_effects=True, vmem_limit_bytes=48 * 1024 * 1024),
            name="lightning_backward",
        )(decay_rate, queries, key_vectors, value_vectors, out_grad, out_weight)

    tok = P("ctx", "head")
    return jax.shard_map(
        local, mesh=mesh, in_specs=(tok, tok, tok, tok, P(None, "head"), P("head")),
        out_specs=(tok, tok, tok, tok), check_vma=False)
```

time: 487 us -> 69 us (0.14)
  waiting for transfers between devices: 327 us -> 0 us
  blocking collectives: 75.7 us -> 0 us
  Pallas kernels: 0 us -> 60.1 us
  other arithmetic: 33.9 us -> 0 us
  matrix products: 15.1 us -> 0 us
  between operations: 14.6 us -> 0.65 us
  local copies, waits for them, and re-layouts: 17.9 us -> 7 us
    unnamed x5 -> x0, waiting for transfers between devices: 203 us -> none
    all_gather x3 -> x0, waiting for transfers between devices: 124 us -> none  [the longest x2 98.2 us: entering(): gathered = jax.tree.map(lambda a: lax.all_gather(a, axis), part)]
    unnamed x1 -> x0, blocking collectives: 75.7 us -> none
    pallas_call x0 -> x1, Pallas kernels: none -> 60.1 us  [local(): pl.pallas_call(functools.partial(kernel, Z, Y), out_shape=[jax.ShapeDtype...]
    add x31 -> x0, other arithmetic: 33 us -> none  [chain_link(): later[0][:, None, None] * earlier[1] + later[1]]
    dot_general x14 -> x0, matrix products: 15.1 us -> none  [the longest x1 6.26 us: local(): lax.dot_general(full_grad, attention_bf, (((0,), (0,)), ((), ())), prefer...]
    unnamed x12 -> x14, local copies, waits for them, and re-layouts: 16.2 us -> 7 us
  transfers between devices with their start and end apart: 4 -> 0, of which waited for: 4 -> 0; matrix products, arithmetic and copies ran while one was open for 14% -> 0% of each run, Pallas kernels for 0% -> 0%
where the time goes in v1:
time: 69 us; the launch traced here: 67.8 us
  Pallas kernels  60.1 us (87%)
  local copies, waits for them, and re-layouts  7 us (10%)
    pallas_call x1, Pallas kernels, local(): pl.pallas_call(functools.partial(kernel, Z, Y), out_shape=[jax.ShapeDtype...  60.1 us
    unnamed x14, local copies, waits for them, and re-layouts  7 us

profile of v1, /device:TPU:16, one launch (start us, length us, event | category | flops | bytes accessed | tf_op | source)
XLA Modules:
  0.0 67.8 jit_solution(14809963577696499256)
XLA Ops:
  0.6 0.0 copy-start
  0.6 0.9 %copy-done = bf16[128,768]{1,0:T(8,128)(2,1)S(1)} copy-done((bf16[128,768]{1,0:T(8,128)(2,1)S(1)}, bf16[128,768]{1,0:T(8,128)(2,1)}, u32[]{:S(2)}) %copy-start) | copy-done | bytes 196632
  1.6 0.0 copy-start.1
  1.6 0.9 %copy-done.1 = bf16[128,512]{1,0:T(8,128)(2,1)S(1)} copy-done((bf16[128,512]{1,0:T(8,128)(2,1)S(1)}, bf16[128,512]{1,0:T(8,128)(2,1)}, u32[]{:S(2)}) %copy-start.1) | copy-done | bytes 131096
  2.5 0.0 copy-start.2
  2.5 0.9 %copy-done.2 = bf16[128,512]{1,0:T(8,128)(2,1)S(1)} copy-done((bf16[128,512]{1,0:T(8,128)(2,1)S(1)}, bf16[128,512]{1,0:T(8,128)(2,1)}, u32[]{:S(2)}) %copy-start.2) | copy-done | bytes 131096
  3.4 0.0 copy-start.3
  3.4 0.9 %copy-done.3 = bf16[128,512]{1,0:T(8,128)(2,1)S(1)} copy-done((bf16[128,512]{1,0:T(8,128)(2,1)S(1)}, bf16[128,512]{1,0:T(8,128)(2,1)}, u32[]{:S(2)}) %copy-start.3) | copy-done | bytes 131096
  4.3 0.0 copy-start.4
  4.3 0.7 copy-done.4
  4.9 60.1 %lightning_backward.1 = (bf16[128,512]{1,0:T(8,128)(2,1)S(1)}, bf16[128,512]{1,0:T(8,128)(2,1)S(1)}, bf16[128,512]{1,0:T(8,128)(2,1)S(1)}, f32[192,512]{1,0:T(8,128)S(1)}) custom-call(f32[4]{0:T(128)S(1)} %copy-done.4, bf16[128,512]{1,0:T(8,128)(2,1)S(1)} %copy-done.1, bf16[128,512]{1,0:T(8,128)(2,1)S(1)} %copy-done.2, bf16[128,512]{1,0:T(8,128)(2,1)S(1)} %copy-done.3, ...), custom_call_target="tpu_custom_call" | custom-call | tf_op jit(solution)/shard_map/lightning_backward/pallas_call | solution.py:328
  65.1 0.7 copy.14
  65.7 0.7 copy.15
  66.4 0.7 copy.16
  67.0 0.7 %copy.17 = f32[192,512]{1,0:T(8,128)} copy(f32[192,512]{1,0:T(8,128)S(1)} %get-tuple-element.11) | data formatting | bytes 786432
Async XLA Ops:
  0.6 0.9 %copy-start = (bf16[128,768]{1,0:T(8,128)(2,1)S(1)}, bf16[128,768]{1,0:T(8,128)(2,1)}, u32[]{:S(2)}) copy-start(bf16[128,768]{1,0:T(8,128)(2,1)} %og_hbm.1) | copy-start | bytes 589828
  1.6 0.9 %copy-start.1 = (bf16[128,512]{1,0:T(8,128)(2,1)S(1)}, bf16[128,512]{1,0:T(8,128)(2,1)}, u32[]{:S(2)}) copy-start(bf16[128,512]{1,0:T(8,128)(2,1)} %q_hbm.1) | copy-start | bytes 393220
  2.5 0.9 %copy-start.2 = (bf16[128,512]{1,0:T(8,128)(2,1)S(1)}, bf16[128,512]{1,0:T(8,128)(2,1)}, u32[]{:S(2)}) copy-start(bf16[128,512]{1,0:T(8,128)(2,1)} %k_hbm.1) | copy-start | bytes 393220
  3.4 0.9 %copy-start.3 = (bf16[128,512]{1,0:T(8,128)(2,1)S(1)}, bf16[128,512]{1,0:T(8,128)(2,1)}, u32[]{:S(2)}) copy-start(bf16[128,512]{1,0:T(8,128)(2,1)} %v_hbm.1) | copy-start | bytes 393220
  4.3 0.7 copy-start.4

commit v2 on v1

v2 whole, which is shorter than its diff:
```python
import functools

import jax
import jax.numpy as jnp
from jax import lax
from jax.experimental import pallas as pl
from jax.experimental.pallas import tpu as pltpu
from jax.sharding import PartitionSpec as P

E = 128
X = 4
MESH = pl.DeviceIdType.MESH
F32 = jnp.float32
BF16 = jnp.bfloat16


def dot(a, b, ca=1, cb=0):
    return lax.dot_general(a, b, (((ca,), (cb,)), ((), ())), preferred_element_type=F32)


def kernel(Z, Y, r_hbm, q_hbm, k_hbm, v_hbm, og_hbm, w_hbm, qg_ref, kg_ref, vg_ref, wg_ref,
           r_ref, q, k, v, w, fg, gz, gzt, hg, hacc, sc, gs, ts, tx, rs, rz, ss, st, acc, ab, dws, dwr, fgp,
           local_sem, g_send, g_recv, p_send, p_recv, t_send, t_recv, r_send, r_recv,
           s_send, s_recv, a_send, a_recv, d_send, d_recv, y_send, y_recv):
    B = q.shape[0]
    D8 = fg.shape[2]
    CH = D8 // X
    H = 2 * Y
    PIECE = B // H
    ctx = lax.axis_index("ctx")
    h = lax.axis_index("head")
    z, x = ctx // X, lax.rem(ctx, X)
    y, c = h // 2, lax.rem(h, 2)

    def at_z(zz):
        return (lax.rem(zz + Z, Z) * X + x, h)

    def at_x(xx):
        return (z * X + xx, h)

    def yhead(dy, cc):
        return lax.rem(y + dy + Y, Y) * 2 + cc

    def at_h(hh):
        return (ctx, hh)

    sib = 1 - c

    def remote(src, dst, send, recv, to):
        return pltpu.make_async_remote_copy(
            src_ref=src, dst_ref=dst, send_sem=send, recv_sem=recv, device_id=to, device_id_type=MESH)

    loads = [pltpu.make_async_copy(a, b, local_sem.at[i]) for i, (a, b) in enumerate(
        ((r_hbm, r_ref), (og_hbm, fg.at[h]), (k_hbm, k), (v_hbm, v), (q_hbm, q), (w_hbm, w)))]
    for load in loads:
        load.start()
    barrier = pltpu.get_barrier_semaphore()
    peers = ([at_z(z + d) for d in range(1, Z)] + [at_x(lax.rem(x + o, X)) for o in range(1, X)]
             + [at_h(lax.rem(h + i, H)) for i in range(1, H)])
    for peer in peers:
        pl.semaphore_signal(barrier, inc=1, device_id=peer, device_id_type=MESH)

    rows = lax.broadcasted_iota(jnp.int32, (B, E), 0).astype(F32)
    dist = (lax.broadcasted_iota(jnp.int32, (B, B), 0)
            - lax.broadcasted_iota(jnp.int32, (B, B), 1)).astype(F32)

    def head(ref, j):
        return ref[:, j * E:(j + 1) * E]

    def weights(j):
        return jnp.where(dist >= 0, jnp.exp(-r_ref[j] * jnp.maximum(dist, 0.0)), 0.0)

    def power(rate, count):
        return jnp.exp(jnp.full((1, E), -rate * count, F32))

    def scan_send(g):
        for o in range(1, X):
            peer = lax.rem(x + o, X)
            remote(ts.at[g, peer], tx.at[g, x], t_send.at[g, o - 1], t_recv.at[g, o - 1], at_x(peer)).start()
        tx[g, x] = ts[g, x]

    def scan_rows(g):
        for o in range(1, X):
            src = lax.rem(x - o + X, X)
            remote(ts.at[g, src], tx.at[g, src], t_send.at[g, o - 1], t_recv.at[g, o - 1], at_x(src)).wait_recv()
        total = jnp.zeros((E, E), F32)
        for xx in range(X):
            away = xx if g else X - 1 - xx
            total = total + power(r_own, float(B * away)) * tx[g, xx].astype(F32)
        rs[g] = total.astype(BF16)
        for d in sorted(range(1, Z), key=lambda d: -min(d, Z - d)):
            there = z - d if g else z + d

            @pl.when((there >= 0) & (there < Z))
            def _():
                remote(rs.at[g], rz.at[g, z], r_send.at[g, d - 1], r_recv.at[g, d - 1], at_z(there)).start()

    def scan_finish(g):
        acc[...] = jnp.zeros((E, E), F32)
        for d in range(1, Z):
            src = z + d if g else z - d

            @pl.when((src >= 0) & (src < Z))
            def _():
                remote(rs.at[g], rz.at[g, src], r_send.at[g, d - 1], r_recv.at[g, d - 1], at_z(src)).wait_recv()
                acc[...] += power(r_own, float(X * B * (d - 1))) * rz[g, src].astype(F32)

        state = acc[...]
        step = power(r_own, float(B))
        for xx in (reversed(range(X)) if g else range(X)):
            ss[g, xx] = state.astype(BF16)
            state = step * state + tx[g, xx].astype(F32)
        for o in range(1, X):
            peer = lax.rem(x + o, X)
            remote(ss.at[g, peer], st.at[g, x], s_send.at[g, o - 1], s_recv.at[g, o - 1], at_x(peer)).start()
        st[g, x] = ss[g, x]

    def scan_wait(g):
        for o in range(1, X):
            src = lax.rem(x - o + X, X)
            remote(ss.at[g, src], st.at[g, src], s_send.at[g, o - 1], s_recv.at[g, o - 1], at_x(src)).wait_recv()

    def piece(n, hh, part_at=None):
        if n == 0:
            if part_at is None:
                return fg.at[hh]
            return fg.at[hh, part_at * (B // 4):(part_at + 1) * (B // 4), :]
        mine = pl.ds(pl.multiple_of(hh * PIECE, PIECE), PIECE)
        if part_at is None:
            return gz.at[:, mine, :]
        return gz.at[part_at * (Z // 4):(part_at + 1) * (Z // 4), mine, :]

    def hop(n, hh, part_at, i, to):
        ref = piece(n, hh, part_at)
        return remote(ref, ref, g_send.at[n, i], g_recv.at[n, i], at_h(to))

    up, down = yhead(1, c), yhead(-1, c)
    far = yhead(2, c)
    across = yhead(0, sib)

    def gather_start(n):
        for u, d in ((0, 2), (1, 3)):
            hop(n, h, u, u, up).start()
            hop(n, h, d, 4 + d, down).start()
        hop(n, h, None, 12, across).start()

    def gather_more(n):
        for u, d in ((2, 0), (3, 1)):
            hop(n, h, u, u, up).start()
            hop(n, h, d, 4 + d, down).start()

    def gather_forward(n):
        for u, d in ((0, 2), (1, 3)):
            hop(n, down, u, u, up).wait_recv()
            hop(n, down, u, 8 + u, up).start()
            hop(n, up, d, 4 + d, down).wait_recv()
            hop(n, up, d, 8 + d, down).start()

    def gather_near(n):
        for u, d in ((2, 0), (3, 1)):
            hop(n, down, u, u, up).wait_recv()
            hop(n, up, d, 4 + d, down).wait_recv()
        hop(n, down, None, 13, across).start()
        hop(n, up, None, 14, across).start()

    def gather_far(n):
        for i in range(4):
            hop(n, far, i, 8 + i, up).wait_recv()
        hop(n, far, None, 15, across).start()

    def gather_across(n, i):
        hh = yhead((0, -1, 1, 2)[i], sib)
        hop(n, hh, None, 12 + i, across).wait_recv()
        return hh

    my_piece = pl.ds(pl.multiple_of(h * PIECE, PIECE), PIECE)

    last = Z // 2 - 1

    def ring_copy(p, way, s, block):
        if s > last - 1:
            ref = ab.at[p, block, way * (B // 2):(way + 1) * (B // 2), :]
            there = z - 2 if way else z + 2
        else:
            ref = ab.at[p, block]
            there = z - 1 if way else z + 1
        return remote(ref, ref, a_send.at[p, way, s], a_recv.at[p, way, s], at_z(there))

    def ring(s, p):
        for way in range(2):
            block = lax.rem(z + (s if way else -s) + Z, Z)
            if s > 0:
                ring_copy(p, way, s - 1, block).wait_recv()
            if s < last:
                ring_copy(p, way, s, block).start()
            if s == last - 1:
                ring_copy(p, way, last, block).start()
            if s == last:
                ring_copy(p, way, last, lax.rem(z + Z // 2, Z)).wait_recv()

    places = ((0, sib), (1, c), (1, sib), (-1, c), (-1, sib), (2, c), (2, sib))

    def spread_piece():
        for dy, cc in places:
            hh = yhead(dy, cc)
            remote(fg.at[h, pl.ds(pl.multiple_of(hh * PIECE, PIECE), PIECE), :], fgp.at[h],
                   y_send.at[hh], y_recv.at[h], at_h(hh)).start()
        fgp[h] = fg[h, my_piece, :]

    def pass_piece(zz):
        @pl.when(zz != z)
        def _():
            remote(fgp.at[zz], gz.at[z, my_piece, :], p_send.at[zz], p_recv.at[z], at_z(zz)).start()

        @pl.when(zz == z)
        def _():
            gz[z, my_piece, :] = fgp[zz]

    def pass_pieces():
        for dy, cc in places:
            hh = yhead(dy, cc)
            remote(fgp.at[hh], fgp.at[hh], y_send.at[hh], y_recv.at[hh], at_h(hh)).wait_recv()
            pass_piece(hh)

    for load in loads[:5]:
        load.wait()
    r_own = r_ref[x]
    for j in range(X):
        decayed = (head(k, j).astype(F32) * jnp.exp(-r_ref[j] * (B - 1.0 - rows))).astype(BF16)
        ts[0, j] = dot(decayed, head(v, j), 0, 0).astype(BF16)
    for j in range(X):
        sc[j] = (dot(head(q, j), head(k, j), 1, 1) * weights(j)).astype(BF16)
    pl.semaphore_wait(barrier, len(peers))

    scan_send(0)
    spread_piece()
    gather_start(0)
    pass_piece(h)
    scan_rows(0)
    pass_pieces()
    gather_more(0)
    gather_forward(0)
    gather_near(0)
    scan_finish(0)
    gather_far(0)
    for zz in range(Z):
        @pl.when(zz != z)
        def _():
            remote(gz.at[zz, my_piece, :], gz.at[zz, my_piece, :], p_send.at[zz], p_recv.at[zz], at_z(zz)).wait_recv()
    gather_start(1)
    for i in range(4):
        gather_across(0, i)

    loads[5].wait()
    hacc[...] = jnp.zeros_like(hacc)

    def part(i, carry):
        hacc[...] += dot(fg[i], w[pl.ds(pl.multiple_of(i * D8, D8), D8), :])
        return carry

    lax.fori_loop(0, H, part, 0)
    hg[...] = hacc[...].astype(BF16)
    gather_more(1)

    scan_wait(0)
    for p in range(2):
        for j in (2 * p, 2 * p + 1):
            inter = jnp.exp(-r_ref[j] * (rows + 1.0)) * dot(head(q, j), st[0, j])
            ab[p, z, :, (j % 2) * E:(j % 2 + 1) * E] = (inter + dot(sc[j], head(v, j))).astype(BF16)
        ring(0, p)
    for j in range(X):
        decayed = (head(q, j).astype(F32) * jnp.exp(-r_ref[j] * rows)).astype(BF16)
        ts[1, j] = dot(decayed, head(hg, j), 0, 0).astype(BF16)
    scan_send(1)
    gather_forward(1)
    ring(1, 0)
    ring(1, 1)
    scan_rows(1)
    for j in range(X):
        gs[j] = (dot(head(hg, j), head(v, j), 1, 1) * weights(j)).astype(BF16)
        inter = jnp.exp(-r_ref[j] * (rows + 1.0)) * dot(head(hg, j), st[0, j], 1, 1)
        qg_ref[:, j * E:(j + 1) * E] = (inter + dot(gs[j], head(k, j))).astype(BF16)
    gather_near(1)
    for s in range(2, last):
        ring(s, 0)
        ring(s, 1)
    gather_far(1)
    for i in range(4):
        gather_across(1, i)
    for zz in range(Z):
        gzt[:, zz * B:(zz + 1) * B] = gz[zz].T
    ring(last, 0)
    ring(last, 1)

    def rows_of(xx):
        return gzt[pl.ds(pl.multiple_of(xx * CH, CH), CH), :]

    def partial(p, xx, half):
        at = lax.rem(xx + X, X) * CH + half * (CH // 2)
        return dot(gzt[pl.ds(pl.multiple_of(at, CH // 2), CH // 2), :], ab[p].reshape(Z * B, 2 * E))

    def share(p, way, i):
        return remote(dws.at[p, way, i], dwr.at[p, way, i], d_send.at[p, way, i], d_recv.at[p, way, i],
                      at_x(lax.rem(x + (X - 1 if way else 1), X)))

    for p in range(2):
        for way in range(2):
            dws[p, way, 0] = partial(p, x + 2, way).astype(BF16)
            share(p, way, 0).start()
        for way in range(2):
            dws[p, way, 1] = partial(p, x + (X - 1 if way else 1), 1 - way).astype(BF16)
            share(p, way, 1).start()
    scan_finish(1)
    for p in range(2):
        for way in range(2):
            own = partial(p, x + (X - 1 if way else 1), way)
            share(p, way, 0).wait_recv()
            dws[p, way, 2] = (own + dwr[p, way, 0].astype(F32)).astype(BF16)
            share(p, way, 2).start()
    for p in range(2):
        for half in range(2):
            wg_ref[half * (CH // 2):(half + 1) * (CH // 2), p * 2 * E:(p + 1) * 2 * E] = partial(p, x, half)
    scan_wait(1)
    for j in range(X):
        back = jnp.exp(-r_ref[j] * (B - rows))
        kg_ref[:, j * E:(j + 1) * E] = (
            back * dot(head(v, j), st[1, j], 1, 1) + dot(gs[j], head(q, j), 0, 0)).astype(BF16)
        vg_ref[:, j * E:(j + 1) * E] = (
            back * dot(head(k, j), st[1, j]) + dot(sc[j], head(hg, j), 0, 0)).astype(BF16)
    for i in (1, 2):
        for p in range(2):
            for way in range(2):
                half = 1 - way if i == 1 else way
                share(p, way, i).wait_recv()
                wg_ref[half * (CH // 2):(half + 1) * (CH // 2), p * 2 * E:(p + 1) * 2 * E] += dwr[p, way, i].astype(F32)

    for g in range(2):
        for o in range(1, X):
            remote(ts.at[g, 0], tx.at[g, 0], t_send.at[g, o - 1], t_recv.at[g, o - 1], at_x(x)).wait_send()
            remote(ss.at[g, 0], st.at[g, 0], s_send.at[g, o - 1], s_recv.at[g, o - 1], at_x(x)).wait_send()
        for d in range(1, Z):
            there = z - d if g else z + d

            @pl.when((there >= 0) & (there < Z))
            def _():
                remote(rs.at[g], rz.at[g, z], r_send.at[g, d - 1], r_recv.at[g, d - 1], at_z(there)).wait_send()
    for n in range(2):
        for i, part_at in enumerate((0, 1, 2, 3) * 3 + (None,) * 4):
            hop(n, h, part_at, i, up).wait_send()
    for zz in range(Z):
        @pl.when(zz != z)
        def _():
            remote(fgp.at[zz], gz.at[z, my_piece, :], p_send.at[zz], p_recv.at[z], at_z(zz)).wait_send()
    for dy, cc in places:
        hh = yhead(dy, cc)
        remote(fgp.at[hh], fgp.at[hh], y_send.at[hh], y_recv.at[hh], at_h(hh)).wait_send()
    for p in range(2):
        for way in range(2):
            for s in range(last + 1):
                ring_copy(p, way, s, z).wait_send()
        for way in range(2):
            for i in range(3):
                share(p, way, i).wait_send()


def store(a, b, c, d, a_out, b_out, c_out, d_out, sem):
    copies = [pltpu.make_async_copy(src, dst, sem.at[i]) for i, (src, dst) in enumerate(
        ((d, d_out), (a, a_out), (b, b_out), (c, c_out)))]
    for copy in copies:
        copy.start()
    for copy in copies:
        copy.wait()


def solution(mesh):
    Z, Y = mesh.shape["ctx"] // X, mesh.shape["head"] // 2
    H = 2 * Y

    def local(queries, key_vectors, value_vectors, out_grad, out_weight, decay_rate):
        B, C = queries.shape
        D8 = out_grad.shape[1]
        D = out_weight.shape[0]
        CH = D8 // X
        dma = pltpu.SemaphoreType.DMA
        vmem = pltpu.VMEM
        hbm = pl.BlockSpec(memory_space=pltpu.HBM)
        results = pl.pallas_call(
            functools.partial(kernel, Z, Y),
            out_shape=[jax.ShapeDtypeStruct((B, C), BF16)] * 3 + [jax.ShapeDtypeStruct((CH, C), F32)],
            in_specs=[hbm] * 6,
            out_specs=[pl.BlockSpec(memory_space=pltpu.VMEM)] * 4,
            scratch_shapes=[
                pltpu.SMEM((X,), F32),
                vmem((B, C), BF16), vmem((B, C), BF16), vmem((B, C), BF16), vmem((D, C), BF16),
                vmem((H, B, D8), BF16), vmem((Z, B, D8), BF16), vmem((D8, Z * B), BF16),
                vmem((B, C), BF16), vmem((B, C), F32),
                vmem((X, B, B), BF16), vmem((X, B, B), BF16),
                vmem((2, X, E, E), BF16), vmem((2, X, E, E), BF16),
                vmem((2, E, E), BF16), vmem((2, Z, E, E), BF16),
                vmem((2, X, E, E), BF16), vmem((2, X, E, E), BF16), vmem((E, E), F32),
                vmem((2, Z, B, 2 * E), BF16),
                vmem((2, 2, 3, CH // 2, 2 * E), BF16), vmem((2, 2, 3, CH // 2, 2 * E), BF16),
                vmem((H, B // H, D8), BF16),
                dma((6,)), dma((2, 16)), dma((2, 16)), dma((Z,)), dma((Z,)),
                dma((2, X - 1)), dma((2, X - 1)), dma((2, Z - 1)), dma((2, Z - 1)),
                dma((2, X - 1)), dma((2, X - 1)), dma((2, 2, Z // 2)), dma((2, 2, Z // 2)),
                dma((2, 2, 3)), dma((2, 2, 3)), dma((H,)), dma((H,)),
            ],
            compiler_params=pltpu.CompilerParams(
                collective_id=0, has_side_effects=True, vmem_limit_bytes=63 * 1024 * 1024),
            name="lightning_backward",
        )(decay_rate, queries, key_vectors, value_vectors, out_grad, out_weight)
        return pl.pallas_call(
            store,
            out_shape=[jax.ShapeDtypeStruct(a.shape, a.dtype) for a in results],
            in_specs=[pl.BlockSpec(memory_space=pltpu.VMEM)] * 4,
            out_specs=[hbm] * 4,
            scratch_shapes=[dma((4,))],
            name="store_results",
        )(*results)

    tok = P("ctx", "head")
    return jax.shard_map(
        local, mesh=mesh, in_specs=(tok, tok, tok, tok, P(None, "head"), P("head")),
        out_specs=(tok, tok, tok, tok), check_vma=False)
```

time: 69 us -> 61.1 us (0.89); the launches traced: 67.8 us -> 60.9 us
  local copies, waits for them, and re-layouts: 7 us -> 0 us
    unnamed x14 -> x0, local copies, waits for them, and re-layouts: 7 us -> none
    pallas_call x0 -> x1, Pallas kernels: none -> 2.1 us  [local(): pl.pallas_call(store, out_shape=[jax.ShapeDtypeStruct(a.shape, a.dtype) f...]
    pallas_call x1, Pallas kernels: 60.1 us -> 58.2 us  [local(): pl.pallas_call(functools.partial(kernel, Z, Y), out_shape=[jax.ShapeDtype...]
where the time goes in v2:
time: 61.1 us; the launch traced here: 60.9 us
  Pallas kernels  60.3 us (99%)
  between operations  0.64 us (1%)
    pallas_call x1, Pallas kernels, local(): pl.pallas_call(functools.partial(kernel, Z, Y), out_shape=[jax.ShapeDtype...  58.2 us
    pallas_call x1, Pallas kernels, local(): pl.pallas_call(store, out_shape=[jax.ShapeDtypeStruct(a.shape, a.dtype) f...  2.1 us

profile of v2, /device:TPU:16, one launch (start us, length us, event | category | flops | bytes accessed | tf_op | source)
XLA Modules:
  0.0 60.9 jit_solution(14360275031863350628)
XLA Ops:
  0.6 58.2 %lightning_backward.1 = (bf16[128,512]{1,0:T(8,128)(2,1)}, bf16[128,512]{1,0:T(8,128)(2,1)}, bf16[128,512]{1,0:T(8,128)(2,1)}, f32[192,512]{1,0:T(8,128)}) custom-call(f32[4]{0:T(128)} %r_hbm.1, bf16[128,512]{1,0:T(8,128)(2,1)} %q_hbm.1, bf16[128,512]{1,0:T(8,128)(2,1)} %k_hbm.1, bf16[128,512]{1,0:T(8,128)(2,1)} %v_hbm.1, bf16[128,768]{1,0:T(8,128)(2,1)} %og_hbm.1, ...), custom_call_target="tpu_custom_call" | custom-call | tf_op jit(solution)/shard_map/lightning_backward/pallas_call | solution.py:387
  58.8 2.1 %store_results.1 = (bf16[128,512]{1,0:T(8,128)(2,1)}, bf16[128,512]{1,0:T(8,128)(2,1)}, bf16[128,512]{1,0:T(8,128)(2,1)}, f32[192,512]{1,0:T(8,128)}) custom-call(bf16[128,512]{1,0:T(8,128)(2,1)} %get-tuple-element.8.a, bf16[128,512]{1,0:T(8,128)(2,1)} %get-tuple-element.9.b, bf16[128,512]{1,0:T(8,128)(2,1)} %get-tuple-element.10.c, ...), custom_call_target="tpu_custom_call" | custom-call | tf_op jit(solution)/shard_map/store_results/pallas_call | solution.py:413

commit v3 on v2

--- a/solution.py
+++ b/solution.py
@@ -18,10 +18,11 @@
     return lax.dot_general(a, b, (((ca,), (cb,)), ((), ())), preferred_element_type=F32)
 
 
-def kernel(Z, Y, r_hbm, q_hbm, k_hbm, v_hbm, og_hbm, w_hbm, qg_ref, kg_ref, vg_ref, wg_ref,
+def kernel(Z, Y, r_hbm, q_hbm, k_hbm, v_hbm, og_hbm, w_hbm, qg_hbm, kg_hbm, vg_hbm, wg_hbm,
            r_ref, q, k, v, w, fg, gz, gzt, hg, hacc, sc, gs, ts, tx, rs, rz, ss, st, acc, ab, dws, dwr, fgp,
+           qg_ref, kg_ref, vg_ref, wg_ref, decay, intra,
            local_sem, g_send, g_recv, p_send, p_recv, t_send, t_recv, r_send, r_recv,
-           s_send, s_recv, a_send, a_recv, d_send, d_recv, y_send, y_recv):
+           s_send, s_recv, a_send, a_recv, d_send, d_recv, y_send, y_recv, out_sem):
     B = q.shape[0]
     D8 = fg.shape[2]
     CH = D8 // X
@@ -86,7 +87,7 @@
         total = jnp.zeros((E, E), F32)
         for xx in range(X):
             away = xx if g else X - 1 - xx
-            total = total + power(r_own, float(B * away)) * tx[g, xx].astype(F32)
+            total = total + row_power[away] * tx[g, xx].astype(F32)
         rs[g] = total.astype(BF16)
         for d in sorted(range(1, Z), key=lambda d: -min(d, Z - d)):
             there = z - d if g else z + d
@@ -103,13 +104,12 @@
             @pl.when((src >= 0) & (src < Z))
             def _():
                 remote(rs.at[g], rz.at[g, src], r_send.at[g, d - 1], r_recv.at[g, d - 1], at_z(src)).wait_recv()
-                acc[...] += power(r_own, float(X * B * (d - 1))) * rz[g, src].astype(F32)
+                acc[...] += z_power[d - 1] * rz[g, src].astype(F32)
 
         state = acc[...]
-        step = power(r_own, float(B))
         for xx in (reversed(range(X)) if g else range(X)):
             ss[g, xx] = state.astype(BF16)
-            state = step * state + tx[g, xx].astype(F32)
+            state = row_power[1] * state + tx[g, xx].astype(F32)
         for o in range(1, X):
             peer = lax.rem(x + o, X)
             remote(ss.at[g, peer], st.at[g, x], s_send.at[g, o - 1], s_recv.at[g, o - 1], at_x(peer)).start()
@@ -225,6 +225,8 @@
     for load in loads[:5]:
         load.wait()
     r_own = r_ref[x]
+    row_power = [power(r_own, float(B * i)) for i in range(X)]
+    z_power = [power(r_own, float(X * B * i)) for i in range(Z - 1)]
     for j in range(X):
         decayed = (head(k, j).astype(F32) * jnp.exp(-r_ref[j] * (B - 1.0 - rows))).astype(BF16)
         ts[0, j] = dot(decayed, head(v, j), 0, 0).astype(BF16)
@@ -232,69 +234,6 @@
         sc[j] = (dot(head(q, j), head(k, j), 1, 1) * weights(j)).astype(BF16)
     pl.semaphore_wait(barrier, len(peers))
 
-    scan_send(0)
-    spread_piece()
-    gather_start(0)
-    pass_piece(h)
-    scan_rows(0)
-    pass_pieces()
-    gather_more(0)
-    gather_forward(0)
-    gather_near(0)
-    scan_finish(0)
-    gather_far(0)
-    for zz in range(Z):
-        @pl.when(zz != z)
-        def _():
-            remote(gz.at[zz, my_piece, :], gz.at[zz, my_piece, :], p_send.at[zz], p_recv.at[zz], at_z(zz)).wait_recv()
-    gather_start(1)
-    for i in range(4):
-        gather_across(0, i)
-
-    loads[5].wait()
-    hacc[...] = jnp.zeros_like(hacc)
-
-    def part(i, carry):
-        hacc[...] += dot(fg[i], w[pl.ds(pl.multiple_of(i * D8, D8), D8), :])
-        return carry
-
-    lax.fori_loop(0, H, part, 0)
-    hg[...] = hacc[...].astype(BF16)
-    gather_more(1)
-
-    scan_wait(0)
-    for p in range(2):
-        for j in (2 * p, 2 * p + 1):
-            inter = jnp.exp(-r_ref[j] * (rows + 1.0)) * dot(head(q, j), st[0, j])
-            ab[p, z, :, (j % 2) * E:(j % 2 + 1) * E] = (inter + dot(sc[j], head(v, j))).astype(BF16)
-        ring(0, p)
-    for j in range(X):
-        decayed = (head(q, j).astype(F32) * jnp.exp(-r_ref[j] * rows)).astype(BF16)
-        ts[1, j] = dot(decayed, head(hg, j), 0, 0).astype(BF16)
-    scan_send(1)
-    gather_forward(1)
-    ring(1, 0)
-    ring(1, 1)
-    scan_rows(1)
-    for j in range(X):
-        gs[j] = (dot(head(hg, j), head(v, j), 1, 1) * weights(j)).astype(BF16)
-        inter = jnp.exp(-r_ref[j] * (rows + 1.0)) * dot(head(hg, j), st[0, j], 1, 1)
-        qg_ref[:, j * E:(j + 1) * E] = (inter + dot(gs[j], head(k, j))).astype(BF16)
-    gather_near(1)
-    for s in range(2, last):
-        ring(s, 0)
-        ring(s, 1)
-    gather_far(1)
-    for i in range(4):
-        gather_across(1, i)
-    for zz in range(Z):
-        gzt[:, zz * B:(zz + 1) * B] = gz[zz].T
-    ring(last, 0)
-    ring(last, 1)
-
-    def rows_of(xx):
-        return gzt[pl.ds(pl.multiple_of(xx * CH, CH), CH), :]
-
     def partial(p, xx, half):
         at = lax.rem(xx + X, X) * CH + half * (CH // 2)
         return dot(gzt[pl.ds(pl.multiple_of(at, CH // 2), CH // 2), :], ab[p].reshape(Z * B, 2 * E))
@@ -303,38 +242,97 @@
         return remote(dws.at[p, way, i], dwr.at[p, way, i], d_send.at[p, way, i], d_recv.at[p, way, i],
                       at_x(lax.rem(x + (X - 1 if way else 1), X)))
 
-    for p in range(2):
+    def wait_pieces():
+        for zz in range(Z):
+            @pl.when(zz != z)
+            def _():
+                remote(gz.at[zz, my_piece, :], gz.at[zz, my_piece, :], p_send.at[zz], p_recv.at[zz], at_z(zz)).wait_recv()
+
+    def from_sibling(n, *which):
+        for i in which:
+            gather_across(n, i)
+
+    def head_grad_part(*distances):
+        for dy in distances:
+            for cc in range(2):
+                hh = yhead(dy, cc)
+                hacc[...] += dot(fg[hh], w[pl.ds(pl.multiple_of(hh * D8, D8), D8), :])
+
+    def head_grad_start():
+        loads[5].wait()
+        hacc[...] = jnp.zeros_like(hacc)
+        head_grad_part(0)
+
+    def head_grad_end():
+        head_grad_part(2)
+        hg[...] = hacc[...].astype(BF16)
+
+    def attention_start():
+        for j in range(X):
+            decay[j] = jnp.exp(-r_ref[j] * (rows + 1.0))
+            intra[0, j] = dot(sc[j], head(v, j))
+
+    def attention(p):
+        for j in (2 * p, 2 * p + 1):
+            inter = decay[j] * dot(head(q, j), st[0, j])
+            ab[p, z, :, (j % 2) * E:(j % 2 + 1) * E] = (inter + intra[0, j]).astype(BF16)
+        ring(0, p)
+
+    def query_terms():
+        for j in range(X):
+            decayed = (head(q, j).astype(F32) * jnp.exp(-r_ref[j] * rows)).astype(BF16)
+            ts[1, j] = dot(decayed, head(hg, j), 0, 0).astype(BF16)
+
+    def query_grads():
+        for j in range(X):
+            gs[j] = (dot(head(hg, j), head(v, j), 1, 1) * weights(j)).astype(BF16)
+            inter = decay[j] * dot(head(hg, j), st[0, j], 1, 1)
+            qg_ref[:, j * E:(j + 1) * E] = (inter + dot(gs[j], head(k, j))).astype(BF16)
+
+    def turn():
+        for zz in range(Z):
+            gzt[:, zz * B:(zz + 1) * B] = gz[zz].T
+
+    def share_first(p):
         for way in range(2):
             dws[p, way, 0] = partial(p, x + 2, way).astype(BF16)
             share(p, way, 0).start()
         for way in range(2):
             dws[p, way, 1] = partial(p, x + (X - 1 if way else 1), 1 - way).astype(BF16)
             share(p, way, 1).start()
-    scan_finish(1)
-    for p in range(2):
+
+    def share_second(p):
         for way in range(2):
             own = partial(p, x + (X - 1 if way else 1), way)
             share(p, way, 0).wait_recv()
             dws[p, way, 2] = (own + dwr[p, way, 0].astype(F32)).astype(BF16)
             share(p, way, 2).start()
-    for p in range(2):
-        for half in range(2):
-            wg_ref[half * (CH // 2):(half + 1) * (CH // 2), p * 2 * E:(p + 1) * 2 * E] = partial(p, x, half)
-    scan_wait(1)
-    for j in range(X):
-        back = jnp.exp(-r_ref[j] * (B - rows))
-        kg_ref[:, j * E:(j + 1) * E] = (
-            back * dot(head(v, j), st[1, j], 1, 1) + dot(gs[j], head(q, j), 0, 0)).astype(BF16)
-        vg_ref[:, j * E:(j + 1) * E] = (
-            back * dot(head(k, j), st[1, j]) + dot(sc[j], head(hg, j), 0, 0)).astype(BF16)
-    for i in (1, 2):
+
+    def share_own():
         for p in range(2):
-            for way in range(2):
-                half = 1 - way if i == 1 else way
-                share(p, way, i).wait_recv()
-                wg_ref[half * (CH // 2):(half + 1) * (CH // 2), p * 2 * E:(p + 1) * 2 * E] += dwr[p, way, i].astype(F32)
-
-    for g in range(2):
+            for half in range(2):
+                wg_ref[half * (CH // 2):(half + 1) * (CH // 2), p * 2 * E:(p + 1) * 2 * E] = partial(p, x, half)
+
+    def key_value_start():
+        for j in range(X):
+            decay[j] = jnp.exp(-r_ref[j] * (B - rows))
+            intra[0, j] = dot(gs[j], head(q, j), 0, 0)
+            intra[1, j] = dot(sc[j], head(hg, j), 0, 0)
+
+    def key_value_grads():
+        for j in range(X):
+            kg_ref[:, j * E:(j + 1) * E] = (
+                decay[j] * dot(head(v, j), st[1, j], 1, 1) + intra[0, j]).astype(BF16)
+            vg_ref[:, j * E:(j + 1) * E] = (
+                decay[j] * dot(head(k, j), st[1, j]) + intra[1, j]).astype(BF16)
+
+    def share_last(i, p):
+        for way in range(2):
+            half = 1 - way if i == 1 else way
+            share(p, way, i).wait_recv()
+            wg_ref[half * (CH // 2):(half + 1) * (CH // 2), p * 2 * E:(p + 1) * 2 * E] += dwr[p, way, i].astype(F32)
+
+    def scan_sent(g):
         for o in range(1, X):
             remote(ts.at[g, 0], tx.at[g, 0], t_send.at[g, o - 1], t_recv.at[g, o - 1], at_x(x)).wait_send()
             remote(ss.at[g, 0], st.at[g, 0], s_send.at[g, o - 1], s_recv.at[g, o - 1], at_x(x)).wait_send()
@@ -344,31 +342,113 @@
             @pl.when((there >= 0) & (there < Z))
             def _():
                 remote(rs.at[g], rz.at[g, z], r_send.at[g, d - 1], r_recv.at[g, d - 1], at_z(there)).wait_send()
-    for n in range(2):
+
+    def gather_sent(n):
         for i, part_at in enumerate((0, 1, 2, 3) * 3 + (None,) * 4):
             hop(n, h, part_at, i, up).wait_send()
-    for zz in range(Z):
-        @pl.when(zz != z)
-        def _():
-            remote(fgp.at[zz], gz.at[z, my_piece, :], p_send.at[zz], p_recv.at[z], at_z(zz)).wait_send()
-    for dy, cc in places:
-        hh = yhead(dy, cc)
-        remote(fgp.at[hh], fgp.at[hh], y_send.at[hh], y_recv.at[hh], at_h(hh)).wait_send()
+
+    def pieces_sent():
+        for zz in range(Z):
+            @pl.when(zz != z)
+            def _():
+                remote(fgp.at[zz], gz.at[z, my_piece, :], p_send.at[zz], p_recv.at[z], at_z(zz)).wait_send()
+        for dy, cc in places:
+            hh = yhead(dy, cc)
+            remote(fgp.at[hh], fgp.at[hh], y_send.at[hh], y_recv.at[hh], at_h(hh)).wait_send()
+
+    def ring_sent():
+        for p in range(2):
+            for way in range(2):
+                for s in range(last + 1):
+                    ring_copy(p, way, s, z).wait_send()
+
+    wide = [slice(p * 2 * E, (p + 1) * 2 * E) for p in range(2)]
+    outs = [pltpu.make_async_copy(a, b, out_sem.at[i]) for i, (a, b) in enumerate(
+        ((qg_ref, qg_hbm), (kg_ref, kg_hbm), (vg_ref, vg_hbm),
+         (wg_ref.at[:, wide[0]], wg_hbm.at[:, wide[0]]), (wg_ref.at[:, wide[1]], wg_hbm.at[:, wide[1]])))]
+
+    scan_send(0)
+    spread_piece()
+    gather_start(0)
+    pass_piece(h)
+    scan_rows(0)
+    attention_start()
+    pass_pieces()
+    gather_more(0)
+    from_sibling(0, 0)
+    head_grad_start()
+    gather_forward(0)
+    gather_near(0)
+    scan_finish(0)
+    gather_far(0)
+    from_sibling(0, 1, 2)
+    head_grad_part(1, -1)
+    scan_wait(0)
+    attention(0)
+    attention(1)
+    wait_pieces()
+    gather_start(1)
+    from_sibling(0, 3)
+    head_grad_end()
+    query_terms()
+    scan_send(1)
+    gather_more(1)
+    ring(1, 0)
+    ring(1, 1)
+    gather_forward(1)
+    query_grads()
+    outs[0].start()
+    ring(2, 0)
+    ring(2, 1)
+    gather_near(1)
+    scan_rows(1)
+    gather_far(1)
+    scan_sent(0)
+    gather_sent(0)
+    key_value_start()
+    from_sibling(1, 0, 1, 2, 3)
+    turn()
+    ring(3, 0)
+    ring(3, 1)
+    share_first(0)
+    share_first(1)
+    scan_finish(1)
+    share_second(0)
+    share_second(1)
+    share_own()
+    pieces_sent()
+    gather_sent(1)
+    ring_sent()
+    scan_wait(1)
+    key_value_grads()
+    share_last(1, 0)
+    share_last(1, 1)
+    outs[1].start()
+    outs[2].start()
+    share_last(2, 0)
+    outs[3].start()
+    share_last(2, 1)
+    outs[4].start()
+
+    scan_sent(1)
     for p in range(2):
-        for way in range(2):
-            for s in range(last + 1):
-                ring_copy(p, way, s, z).wait_send()
         for way in range(2):
             for i in range(3):
                 share(p, way, i).wait_send()
-
-
-def store(a, b, c, d, a_out, b_out, c_out, d_out, sem):
-    copies = [pltpu.make_async_copy(src, dst, sem.at[i]) for i, (src, dst) in enumerate(
-        ((d, d_out), (a, a_out), (b, b_out), (c, c_out)))]
-    for copy in copies:
+    for copy in outs:
+        copy.wait()
+
+
+def store(*refs):
+    results, outs, held, in_sem, out_sem = refs[:4], refs[4:8], refs[8:12], refs[12], refs[13]
+    loads = [pltpu.make_async_copy(a, b, in_sem.at[i]) for i, (a, b) in enumerate(zip(results, held))]
+    stores = [pltpu.make_async_copy(a, b, out_sem.at[i]) for i, (a, b) in enumerate(zip(held, outs))]
+    for load in loads:
+        load.start()
+    for load, copy in zip(loads, stores):
+        load.wait()
         copy.start()
-    for copy in copies:
+    for copy in stores:
         copy.wait()
 
 
@@ -388,7 +468,7 @@
             functools.partial(kernel, Z, Y),
             out_shape=[jax.ShapeDtypeStruct((B, C), BF16)] * 3 + [jax.ShapeDtypeStruct((CH, C), F32)],
             in_specs=[hbm] * 6,
-            out_specs=[pl.BlockSpec(memory_space=pltpu.VMEM)] * 4,
+            out_specs=[hbm] * 4,
             scratch_shapes=[
                 pltpu.SMEM((X,), F32),
                 vmem((B, C), BF16), vmem((B, C), BF16), vmem((B, C), BF16), vmem((D, C), BF16),
@@ -401,10 +481,12 @@
                 vmem((2, Z, B, 2 * E), BF16),
                 vmem((2, 2, 3, CH // 2, 2 * E), BF16), vmem((2, 2, 3, CH // 2, 2 * E), BF16),
                 vmem((H, B // H, D8), BF16),
+                vmem((B, C), BF16), vmem((B, C), BF16), vmem((B, C), BF16), vmem((CH, C), F32),
+                vmem((X, B, E), F32), vmem((2, X, B, E), F32),
                 dma((6,)), dma((2, 16)), dma((2, 16)), dma((Z,)), dma((Z,)),
                 dma((2, X - 1)), dma((2, X - 1)), dma((2, Z - 1)), dma((2, Z - 1)),
                 dma((2, X - 1)), dma((2, X - 1)), dma((2, 2, Z // 2)), dma((2, 2, Z // 2)),
-                dma((2, 2, 3)), dma((2, 2, 3)), dma((H,)), dma((H,)),
+                dma((2, 2, 3)), dma((2, 2, 3)), dma((H,)), dma((H,)), dma((5,)),
             ],
             compiler_params=pltpu.CompilerParams(
                 collective_id=0, has_side_effects=True, vmem_limit_bytes=63 * 1024 * 1024),
@@ -413,9 +495,10 @@
         return pl.pallas_call(
             store,
             out_shape=[jax.ShapeDtypeStruct(a.shape, a.dtype) for a in results],
-            in_specs=[pl.BlockSpec(memory_space=pltpu.VMEM)] * 4,
+            in_specs=[hbm] * 4,
             out_specs=[hbm] * 4,
-            scratch_shapes=[dma((4,))],
+            scratch_shapes=[vmem(a.shape, a.dtype) for a in results] + [dma((4,)), dma((4,))],
+            compiler_params=pltpu.CompilerParams(vmem_limit_bytes=63 * 1024 * 1024),
             name="store_results",
         )(*results)
 

time: 61.1 us -> 57.5 us (0.941)
  Pallas kernels: 60.3 us -> 56.4 us
    pallas_call x1, Pallas kernels: 58.2 us -> 54.4 us  [local(): pl.pallas_call(functools.partial(kernel, Z, Y), out_shape=[jax.ShapeDtype...]
where the time goes in v3:
time: 57.5 us; the launch traced here: 57.1 us
  Pallas kernels  56.4 us (98%)
  between operations  0.64 us (1%)
    pallas_call x1, Pallas kernels, local(): pl.pallas_call(functools.partial(kernel, Z, Y), out_shape=[jax.ShapeDtype...  54.4 us
    pallas_call x1, Pallas kernels, local(): pl.pallas_call(store, out_shape=[jax.ShapeDtypeStruct(a.shape, a.dtype) f...  2.01 us

profile of v3, /device:TPU:16, one launch (start us, length us, event | category | flops | bytes accessed | tf_op | source)
XLA Modules:
  0.0 57.1 jit_solution(15882417778806982530)
XLA Ops:
  0.6 54.4 %lightning_backward.1 = (bf16[128,512]{1,0:T(8,128)(2,1)}, bf16[128,512]{1,0:T(8,128)(2,1)}, bf16[128,512]{1,0:T(8,128)(2,1)}, f32[192,512]{1,0:T(8,128)}) custom-call(f32[4]{0:T(128)} %r_hbm.1, bf16[128,512]{1,0:T(8,128)(2,1)} %q_hbm.1, bf16[128,512]{1,0:T(8,128)(2,1)} %k_hbm.1, bf16[128,512]{1,0:T(8,128)(2,1)} %v_hbm.1, bf16[128,768]{1,0:T(8,128)(2,1)} %og_hbm.1, ...), custom_call_target="tpu_custom_call" | custom-call | tf_op jit(solution)/shard_map/lightning_backward/pallas_call | solution.py:467
  55.1 2.0 %store_results.1 = (bf16[128,512]{1,0:T(8,128)(2,1)}, bf16[128,512]{1,0:T(8,128)(2,1)}, bf16[128,512]{1,0:T(8,128)(2,1)}, f32[192,512]{1,0:T(8,128)}) custom-call(bf16[128,512]{1,0:T(8,128)(2,1)} %get-tuple-element.8.refs_0_, bf16[128,512]{1,0:T(8,128)(2,1)} %get-tuple-element.9.refs_1_, bf16[128,512]{1,0:T(8,128)(2,1)} %get-tuple-element.10.refs_2_, ...), custom_call_target="tpu_custom_call" | custom-call | tf_op jit(solution)/shard_map/store_results/pallas_call | solution.py:495

commit v4 on v3

--- a/solution.py
+++ b/solution.py
@@ -46,13 +46,14 @@
         return (ctx, hh)
 
     sib = 1 - c
+    half = Z // 2
 
     def remote(src, dst, send, recv, to):
         return pltpu.make_async_remote_copy(
             src_ref=src, dst_ref=dst, send_sem=send, recv_sem=recv, device_id=to, device_id_type=MESH)
 
     loads = [pltpu.make_async_copy(a, b, local_sem.at[i]) for i, (a, b) in enumerate(
-        ((r_hbm, r_ref), (og_hbm, fg.at[h]), (k_hbm, k), (v_hbm, v), (q_hbm, q), (w_hbm, w)))]
+        ((r_hbm, r_ref), (k_hbm, k), (v_hbm, v), (og_hbm, fg.at[h]), (q_hbm, q), (w_hbm, w)))]
     for load in loads:
         load.start()
     barrier = pltpu.get_barrier_semaphore()
@@ -91,20 +92,40 @@
         rs[g] = total.astype(BF16)
         for d in sorted(range(1, Z), key=lambda d: -min(d, Z - d)):
             there = z - d if g else z + d
-
-            @pl.when((there >= 0) & (there < Z))
+            now = (there // half == z // half) if g else True
+
+            @pl.when((there >= 0) & (there < Z) & now)
             def _():
-                remote(rs.at[g], rz.at[g, z], r_send.at[g, d - 1], r_recv.at[g, d - 1], at_z(there)).start()
+                send_row(g, d, there)
+
+    def send_row(g, d, there):
+        remote(rs.at[g], rz.at[g, z], r_send.at[g, d - 1], r_recv.at[g, d - 1], at_z(there)).start()
+
+    def add_row(g, d, src):
+        remote(rs.at[g], rz.at[g, src], r_send.at[g, d - 1], r_recv.at[g, d - 1], at_z(src)).wait_recv()
+        acc[...] += z_power[d - 1] * rz[g, src].astype(F32)
+
+    def scan_mid(g):
+        acc[...] = jnp.zeros((E, E), F32)
+
+        @pl.when(z == half)
+        def _():
+            for d in range(1, Z - half):
+                add_row(g, d, z + d)
+            rs[g] = (rs[g].astype(F32) + z_power[1] * acc[...]).astype(BF16)
+            for d in range(half, 0, -1):
+                send_row(g, d, z - d)
 
     def scan_finish(g):
-        acc[...] = jnp.zeros((E, E), F32)
+        if g == 0:
+            acc[...] = jnp.zeros((E, E), F32)
         for d in range(1, Z):
             src = z + d if g else z - d
-
-            @pl.when((src >= 0) & (src < Z))
+            now = ((src // half == z // half) | (src == half)) & (z != half) if g else True
+
+            @pl.when((src >= 0) & (src < Z) & now)
             def _():
-                remote(rs.at[g], rz.at[g, src], r_send.at[g, d - 1], r_recv.at[g, d - 1], at_z(src)).wait_recv()
-                acc[...] += z_power[d - 1] * rz[g, src].astype(F32)
+                add_row(g, d, src)
 
         state = acc[...]
         for xx in (reversed(range(X)) if g else range(X)):
@@ -222,7 +243,7 @@
             remote(fgp.at[hh], fgp.at[hh], y_send.at[hh], y_recv.at[hh], at_h(hh)).wait_recv()
             pass_piece(hh)
 
-    for load in loads[:5]:
+    for load in loads[:4]:
         load.wait()
     r_own = r_ref[x]
     row_power = [power(r_own, float(B * i)) for i in range(X)]
@@ -230,12 +251,10 @@
     for j in range(X):
         decayed = (head(k, j).astype(F32) * jnp.exp(-r_ref[j] * (B - 1.0 - rows))).astype(BF16)
         ts[0, j] = dot(decayed, head(v, j), 0, 0).astype(BF16)
-    for j in range(X):
-        sc[j] = (dot(head(q, j), head(k, j), 1, 1) * weights(j)).astype(BF16)
     pl.semaphore_wait(barrier, len(peers))
 
-    def partial(p, xx, half):
-        at = lax.rem(xx + X, X) * CH + half * (CH // 2)
+    def partial(p, xx, part_at):
+        at = lax.rem(xx + X, X) * CH + part_at * (CH // 2)
         return dot(gzt[pl.ds(pl.multiple_of(at, CH // 2), CH // 2), :], ab[p].reshape(Z * B, 2 * E))
 
     def share(p, way, i):
@@ -267,6 +286,11 @@
         head_grad_part(2)
         hg[...] = hacc[...].astype(BF16)
 
+    def attention_scores():
+        loads[4].wait()
+        for j in range(X):
+            sc[j] = (dot(head(q, j), head(k, j), 1, 1) * weights(j)).astype(BF16)
+
     def attention_start():
         for j in range(X):
             decay[j] = jnp.exp(-r_ref[j] * (rows + 1.0))
@@ -297,6 +321,8 @@
         for way in range(2):
             dws[p, way, 0] = partial(p, x + 2, way).astype(BF16)
             share(p, way, 0).start()
+
+    def share_direct(p):
         for way in range(2):
             dws[p, way, 1] = partial(p, x + (X - 1 if way else 1), 1 - way).astype(BF16)
             share(p, way, 1).start()
@@ -310,8 +336,8 @@
 
     def share_own():
         for p in range(2):
-            for half in range(2):
-                wg_ref[half * (CH // 2):(half + 1) * (CH // 2), p * 2 * E:(p + 1) * 2 * E] = partial(p, x, half)
+            for part_at in range(2):
+                wg_ref[part_at * (CH // 2):(part_at + 1) * (CH // 2), p * 2 * E:(p + 1) * 2 * E] = partial(p, x, part_at)
 
     def key_value_start():
         for j in range(X):
@@ -328,9 +354,9 @@
 
     def share_last(i, p):
         for way in range(2):
-            half = 1 - way if i == 1 else way
+            part_at = 1 - way if i == 1 else way
             share(p, way, i).wait_recv()
-            wg_ref[half * (CH // 2):(half + 1) * (CH // 2), p * 2 * E:(p + 1) * 2 * E] += dwr[p, way, i].astype(F32)
+            wg_ref[part_at * (CH // 2):(part_at + 1) * (CH // 2), p * 2 * E:(p + 1) * 2 * E] += dwr[p, way, i].astype(F32)
 
     def scan_sent(g):
         for o in range(1, X):
@@ -338,8 +364,9 @@
             remote(ss.at[g, 0], st.at[g, 0], s_send.at[g, o - 1], s_recv.at[g, o - 1], at_x(x)).wait_send()
         for d in range(1, Z):
             there = z - d if g else z + d
-
-            @pl.when((there >= 0) & (there < Z))
+            ever = (there // half == z // half) | (z == half) if g else True
+
+            @pl.when((there >= 0) & (there < Z) & ever)
             def _():
                 remote(rs.at[g], rz.at[g, z], r_send.at[g, d - 1], r_recv.at[g, d - 1], at_z(there)).wait_send()
 
@@ -371,13 +398,14 @@
     spread_piece()
     gather_start(0)
     pass_piece(h)
+    attention_scores()
     scan_rows(0)
     attention_start()
-    pass_pieces()
     gather_more(0)
     from_sibling(0, 0)
     head_grad_start()
     gather_forward(0)
+    pass_pieces()
     gather_near(0)
     scan_finish(0)
     gather_far(0)
@@ -396,12 +424,13 @@
     ring(1, 0)
     ring(1, 1)
     gather_forward(1)
+    scan_rows(1)
     query_grads()
     outs[0].start()
     ring(2, 0)
     ring(2, 1)
     gather_near(1)
-    scan_rows(1)
+    scan_mid(1)
     gather_far(1)
     scan_sent(0)
     gather_sent(0)
@@ -409,9 +438,11 @@
     from_sibling(1, 0, 1, 2, 3)
     turn()
     ring(3, 0)
+    share_first(0)
     ring(3, 1)
-    share_first(0)
     share_first(1)
+    share_direct(0)
+    share_direct(1)
     scan_finish(1)
     share_second(0)
     share_second(1)

time: 57.5 us -> 54.3 us (0.944)
  Pallas kernels: 56.4 us -> 53.6 us
    pallas_call x1, Pallas kernels: 54.4 us -> 51.6 us  [local(): pl.pallas_call(functools.partial(kernel, Z, Y), out_shape=[jax.ShapeDtype...]
where the time goes in v4:
time: 54.3 us; the launch traced here: 54.2 us
  Pallas kernels  53.6 us (99%)
  between operations  0.64 us (1%)
    pallas_call x1, Pallas kernels, local(): pl.pallas_call(functools.partial(kernel, Z, Y), out_shape=[jax.ShapeDtype...  51.6 us
    pallas_call x1, Pallas kernels, local(): pl.pallas_call(store, out_shape=[jax.ShapeDtypeStruct(a.shape, a.dtype) f...  2.01 us

profile of v4, /device:TPU:16, one launch (start us, length us, event | category | flops | bytes accessed | tf_op | source)
XLA Modules:
  0.0 54.2 jit_solution(1104720350367375785)
XLA Ops:
  0.6 51.6 %lightning_backward.1 = (bf16[128,512]{1,0:T(8,128)(2,1)}, bf16[128,512]{1,0:T(8,128)(2,1)}, bf16[128,512]{1,0:T(8,128)(2,1)}, f32[192,512]{1,0:T(8,128)}) custom-call(f32[4]{0:T(128)} %r_hbm.1, bf16[128,512]{1,0:T(8,128)(2,1)} %q_hbm.1, bf16[128,512]{1,0:T(8,128)(2,1)} %k_hbm.1, bf16[128,512]{1,0:T(8,128)(2,1)} %v_hbm.1, bf16[128,768]{1,0:T(8,128)(2,1)} %og_hbm.1, ...), custom_call_target="tpu_custom_call" | custom-call | tf_op jit(solution)/shard_map/lightning_backward/pallas_call | solution.py:498
  52.2 2.0 %store_results.1 = (bf16[128,512]{1,0:T(8,128)(2,1)}, bf16[128,512]{1,0:T(8,128)(2,1)}, bf16[128,512]{1,0:T(8,128)(2,1)}, f32[192,512]{1,0:T(8,128)}) custom-call(bf16[128,512]{1,0:T(8,128)(2,1)} %get-tuple-element.8.refs_0_, bf16[128,512]{1,0:T(8,128)(2,1)} %get-tuple-element.9.refs_1_, bf16[128,512]{1,0:T(8,128)(2,1)} %get-tuple-element.10.refs_2_, ...), custom_call_target="tpu_custom_call" | custom-call | tf_op jit(solution)/shard_map/store_results/pallas_call | solution.py:526

commit v5 on v4

--- a/solution.py
+++ b/solution.py
@@ -427,9 +427,9 @@
     scan_rows(1)
     query_grads()
     outs[0].start()
+    gather_near(1)
     ring(2, 0)
     ring(2, 1)
-    gather_near(1)
     scan_mid(1)
     gather_far(1)
     scan_sent(0)

time: 54.3 us -> 53.8 us (level)
  Pallas kernels: 53.6 us -> 53 us
where the time goes in v5:
time: 53.8 us; the launch traced here: 53.7 us
  Pallas kernels  53 us (99%)
  between operations  0.64 us (1%)
    pallas_call x1, Pallas kernels, local(): pl.pallas_call(functools.partial(kernel, Z, Y), out_shape=[jax.ShapeDtype...  51 us
    pallas_call x1, Pallas kernels, local(): pl.pallas_call(store, out_shape=[jax.ShapeDtypeStruct(a.shape, a.dtype) f...  2.01 us

profile of v5, /device:TPU:16, one launch (start us, length us, event | category | flops | bytes accessed | tf_op | source)
XLA Modules:
  0.0 53.7 jit_solution(16806655472240308719)
XLA Ops:
  0.6 51.0 %lightning_backward.1 = (bf16[128,512]{1,0:T(8,128)(2,1)}, bf16[128,512]{1,0:T(8,128)(2,1)}, bf16[128,512]{1,0:T(8,128)(2,1)}, f32[192,512]{1,0:T(8,128)}) custom-call(f32[4]{0:T(128)} %r_hbm.1, bf16[128,512]{1,0:T(8,128)(2,1)} %q_hbm.1, bf16[128,512]{1,0:T(8,128)(2,1)} %k_hbm.1, bf16[128,512]{1,0:T(8,128)(2,1)} %v_hbm.1, bf16[128,768]{1,0:T(8,128)(2,1)} %og_hbm.1, ...), custom_call_target="tpu_custom_call" | custom-call | tf_op jit(solution)/shard_map/lightning_backward/pallas_call | solution.py:498
  51.7 2.0 %store_results.1 = (bf16[128,512]{1,0:T(8,128)(2,1)}, bf16[128,512]{1,0:T(8,128)(2,1)}, bf16[128,512]{1,0:T(8,128)(2,1)}, f32[192,512]{1,0:T(8,128)}) custom-call(bf16[128,512]{1,0:T(8,128)(2,1)} %get-tuple-element.8.refs_0_, bf16[128,512]{1,0:T(8,128)(2,1)} %get-tuple-element.9.refs_1_, bf16[128,512]{1,0:T(8,128)(2,1)} %get-tuple-element.10.refs_2_, ...), custom_call_target="tpu_custom_call" | custom-call | tf_op jit(solution)/shard_map/store_results/pallas_call | solution.py:526
